TPU v7x, 128 devices: a whole 4x4x4 slice. The times are simulated.
128 devices in a mesh: dp: 8 (over z, y_lo), expert: 16 (over y_hi, x, core).
Axes of the slice: x: 4, y: 4 (y_hi: 2, y_lo: 2; y = y_hi * 2 + y_lo), z: 4, core: 2. Of those that a mesh axis runs over, the one named last changes fastest.
Arguments:
- tokens_in: bfloat16 [16384, 2560], P(('dp', 'expert')), may hold values from -6 to 6
- out_grad: bfloat16 [16384, 2560], P(('dp', 'expert')), may hold values from -6 to 6
- expert_ids: int32 [16384, 6], P(('dp', 'expert')), may hold values from 0 to 15, as said below
- route_probs: bfloat16 [16384, 6], P(('dp', 'expert')), may hold values from 0.019897461 to 0.5
- weights_in: float32 [16, 2560, 1536], P('expert', 'dp'), may hold values from -0.125 to 0.125
- weights_out: float32 [16, 768, 2560], P('expert', 'dp'), may hold values from -0.21875 to 0.21875
- first_in: float32 [16, 2560, 1536], P('expert', 'dp'), may hold values from -24 to 24
- first_out: float32 [16, 768, 2560], P('expert', 'dp'), may hold values from -24 to 24
- second_in: float32 [16, 2560, 1536], P('expert', 'dp'), may hold values from 1 to 100
- second_out: float32 [16, 768, 2560], P('expert', 'dp'), may hold values from 1 to 100
Outputs:
- input_grad: bfloat16 [16384, 2560], P(('dp', 'expert'))
- route_grad: bfloat16 [16384, 6], P(('dp', 'expert'))
- new_weights_in: float32 [16, 2560, 1536], P('expert', 'dp')
- new_weights_out: float32 [16, 768, 2560], P('expert', 'dp')
- new_first_in: float32 [16, 2560, 1536], P('expert', 'dp')
- new_first_out: float32 [16, 768, 2560], P('expert', 'dp')
- new_second_in: float32 [16, 2560, 1536], P('expert', 'dp')
- new_second_out: float32 [16, 768, 2560], P('expert', 'dp')
Inputs may be any that keep to these rules, and one draw needn't show every extreme that they name: `expert_ids`: each row names 6 different experts. Among the rows of one device no expert is named more than 54 times, and in every group of 16 devices that share a dp index one expert is named exactly 54 times by each device of the group.
All inputs are finite; a program needn't handle non-finite values.
Results may differ from a plain program's by a relative error of at most 0.025.
Values may be sent and summed in bfloat16 or wider, within the bound.
No kernel may reach another device: no remote copies, remote signals or barrier semaphores. Data moves between devices by JAX's collectives and lax.ppermute only.
A program may use at most 128 MiB of HBM per device.

v0:
```python
import jax
import jax.numpy as jnp
from jax import lax
from jax.sharding import PartitionSpec as P

beta_one = 0.9
beta_two = 0.95
learn_rate = 0.00024
decay_rate = 0.1
adam_eps = 1e-08
adam_step = 100.0


def silu_parts(gate_value):
    sigmoid_value = jax.nn.sigmoid(gate_value)
    return (gate_value * sigmoid_value, sigmoid_value * (1.0 + gate_value * (1.0 - sigmoid_value)))


def expert_rows(token_block, grad_block, prob_block, wide_in, wide_out):
    hidden = wide_out.shape[0]
    preact = jnp.dot(token_block, wide_in, preferred_element_type=jnp.float32)
    gate_value = preact[:, :hidden]
    up_value = preact[:, hidden:]
    silu_gate, silu_slope = silu_parts(gate_value)
    activation = silu_gate * up_value
    back_proj = lax.dot_general(
        grad_block, wide_out, (((1,), (1,)), ((), ())), preferred_element_type=jnp.float32
    )
    route_part = jnp.sum(activation * back_proj, axis=1).astype(jnp.bfloat16)
    weight = prob_block.astype(jnp.float32)[:, None]
    act_grad = weight * back_proj
    pre_grad = jnp.concatenate(
        [act_grad * up_value * silu_slope, act_grad * silu_gate], axis=1
    ).astype(jnp.bfloat16)
    scaled = (weight * activation).astype(jnp.bfloat16)
    row_grad = lax.dot_general(
        pre_grad, wide_in, (((1,), (1,)), ((), ())), preferred_element_type=jnp.float32
    ).astype(jnp.bfloat16)
    return (row_grad, route_part, pre_grad, scaled)


def adam_update(weights, first, second, grad):
    first_new = beta_one * first + (1.0 - beta_one) * grad
    second_new = beta_two * second + (1.0 - beta_two) * grad * grad
    fix_one = 1.0 - beta_one**adam_step
    fix_two = 1.0 - beta_two**adam_step
    step_size = first_new / fix_one / (jnp.sqrt(second_new / fix_two) + adam_eps)
    return (weights - learn_rate * (step_size + decay_rate * weights), first_new, second_new)


def on_device(
    tokens_in,
    out_grad,
    expert_ids,
    route_probs,
    weights_in,
    weights_out,
    first_in,
    first_out,
    second_in,
    second_out,
):
    experts = lax.axis_size("expert")
    token_count, top_count = expert_ids.shape
    features = tokens_in.shape[1]
    capacity = 9 * token_count * top_count // (8 * experts)
    pick_total = token_count * top_count
    flat_ids = expert_ids.reshape(-1)
    onehot = (flat_ids[:, None] == jnp.arange(experts, dtype=jnp.int32)[None, :]).astype(jnp.int32)
    slot_rank = jnp.sum((jnp.cumsum(onehot, axis=0) - onehot) * onehot, axis=1)
    slot_pick = (
        jnp.full((experts, capacity), pick_total, jnp.int32)
        .at[flat_ids, slot_rank]
        .set(jnp.arange(pick_total, dtype=jnp.int32))
    )
    token_rows = slot_pick // top_count
    zero_row = jnp.zeros((1, features), jnp.bfloat16)
    sent_tokens = jnp.concatenate([tokens_in, zero_row], axis=0)[token_rows]
    sent_grads = jnp.concatenate([out_grad, zero_row], axis=0)[token_rows]
    sent_probs = jnp.concatenate([route_probs.reshape(-1), jnp.zeros((1,), jnp.bfloat16)])[
        slot_pick
    ]
    gathered_in, gathered_out = (
        lax.all_gather(weights_in.astype(jnp.bfloat16), "dp", axis=1, tiled=True),
        lax.all_gather(weights_out.astype(jnp.bfloat16), "dp", axis=1, tiled=True),
    )
    wide_in = gathered_in[0]
    wide_out = gathered_out[0]
    received_tokens, received_grads, received_probs = (
        lax.all_to_all(sent_tokens, "expert", split_axis=0, concat_axis=0, tiled=True),
        lax.all_to_all(sent_grads, "expert", split_axis=0, concat_axis=0, tiled=True),
        lax.all_to_all(sent_probs, "expert", split_axis=0, concat_axis=0, tiled=True),
    )
    sources, block_rows = received_probs.shape
    row_grad, route_part, pre_grad, scaled = expert_rows(
        received_tokens.reshape(sources * block_rows, features),
        received_grads.reshape(sources * block_rows, features),
        received_probs.reshape(sources * block_rows),
        wide_in,
        wide_out,
    )
    row_grad, route_part, pre_grad, scaled = (
        row_grad.reshape(sources, block_rows, features),
        route_part.reshape(sources, block_rows),
        pre_grad.reshape(sources, block_rows, -1),
        scaled.reshape(sources, block_rows, -1),
    )
    back_rows, back_probs = (
        lax.all_to_all(row_grad, "expert", split_axis=0, concat_axis=0, tiled=True),
        lax.all_to_all(route_part, "expert", split_axis=0, concat_axis=0, tiled=True),
    )
    row_total = received_tokens.shape[0] * received_tokens.shape[1]
    flat_tokens = received_tokens.reshape(row_total, features)
    flat_grads = received_grads.reshape(row_total, features)
    flat_pre = pre_grad.reshape(row_total, -1)
    flat_scaled = scaled.reshape(row_total, -1)
    columns = flat_tokens
    grad_in = lax.psum_scatter(
        lax.dot_general(
            columns, flat_pre, (((0,), (0,)), ((), ())), preferred_element_type=jnp.float32
        ).astype(jnp.bfloat16),
        "dp",
        scatter_dimension=0,
        tiled=True,
    ).astype(jnp.float32)
    columns = flat_scaled
    grad_out = lax.psum_scatter(
        lax.dot_general(
            columns, flat_grads, (((0,), (0,)), ((), ())), preferred_element_type=jnp.float32
        ).astype(jnp.bfloat16),
        "dp",
        scatter_dimension=0,
        tiled=True,
    ).astype(jnp.float32)
    new_weights_in, new_first_in, new_second_in = adam_update(
        weights_in, first_in, second_in, grad_in[None]
    )
    new_weights_out, new_first_out, new_second_out = adam_update(
        weights_out, first_out, second_out, grad_out[None]
    )
    gather_index = flat_ids * capacity + slot_rank
    picked = back_rows.reshape(experts * capacity, features)[gather_index]
    input_grad = jnp.sum(
        picked.reshape(token_count, top_count, features), axis=1, dtype=jnp.float32
    ).astype(jnp.bfloat16)
    route_grad = back_probs.reshape(-1)[gather_index].reshape(token_count, top_count)
    return (
        input_grad,
        route_grad,
        new_weights_in,
        new_weights_out,
        new_first_in,
        new_first_out,
        new_second_in,
        new_second_out,
    )


def solution(mesh):
    placed = (
        P(("dp", "expert"), None),
        P(("dp", "expert"), None),
        P(("dp", "expert"), None),
        P(("dp", "expert"), None),
        P("expert", "dp", None),
        P("expert", "dp", None),
        P("expert", "dp", None),
        P("expert", "dp", None),
        P("expert", "dp", None),
        P("expert", "dp", None),
    )
    return jax.shard_map(
        on_device,
        mesh=mesh,
        in_specs=placed,
        out_specs=(
            P(("dp", "expert"), None),
            P(("dp", "expert"), None),
            P("expert", "dp", None),
            P("expert", "dp", None),
            P("expert", "dp", None),
            P("expert", "dp", None),
            P("expert", "dp", None),
            P("expert", "dp", None),
        ),
        check_vma=False,
    )
```

profile of v0, /device:TPU:1, one launch (start us, length us, event | category | flops | bytes accessed | tf_op | source)
XLA Modules:
  0.0 710.2 jit_solution(9112499715180964605)
XLA Ops:
  7.2 0.0 all-gather.5.cloned.1.call-start
  7.2 2.6 convert_element_type.63
  9.8 0.0 all-gather.5.cloned.1.call-update
  9.9 0.1 copy.25
  10.0 0.1 reshape.163
  10.1 0.1 eq.29
  10.3 0.1 eq.25
  10.4 0.1 copy.24
  10.5 0.2 reshape.162
  10.7 1.7 reduce-window.6
  12.4 0.3 slice_reduce_fusion
  12.7 0.1 fusion.21
  12.9 37.7 %scatter_fusion = s32[16,54]{1,0:T(8,128)S(1)} fusion(s32[16,54]{1,0:T(8,128)S(1)} %broadcast_in_dim.6, s32[768]{0:T(1024)S(1)} %get-tuple-element.25, s32[768]{0:T(1024)S(1)} %iota.11), kind=kCustom, calls=%fused_computation.5 | custom fusion | bytes 15360 | tf_op jit(solution)/shard_map/scatter | solution.py:74
  50.6 0.0 copy-start.5
  50.6 0.1 reshape.175
  50.7 5.8 gather_fusion
  56.5 0.7 all_to_all.25
  57.2 8.4 %all-to-all-start = ((bf16[16,1,54]{2,1,0:T(2,128)(2,1)}), bf16[16,1,54]{2,1,0:T(2,128)(2,1)S(1)}, u32[]{:S(2)}, u32[]{:S(2)}) async-start(bf16[16,1,54]{2,1,0:T(2,128)(2,1)} %all_to_all.25), calls=%async_computation | async-start | bytes 16384 | tf_op jit(solution)/shard_map/all_to_all | solution.py:92
  65.7 0.1 reshape.183
  65.8 5.3 gather_fusion.1
  71.2 5.4 reshape.182
  76.5 0.0 all-to-all-done
  76.5 7.4 %all-to-all-start.1 = ((bf16[16,54,2560]{2,1,0:T(8,128)(2,1)}), bf16[16,54,2560]{2,1,0:T(8,128)(2,1)}, u32[]{:S(2)}, u32[]{:S(2)}) async-start(bf16[16,54,2560]{2,1,0:T(8,128)(2,1)} %reshape.182), calls=%async_computation.1 | async-start | bytes 9175040 | tf_op jit(solution)/shard_map/all_to_all | solution.py:91
  83.9 0.0 copy-done.6
  84.0 5.3 gather_fusion.2
  89.3 5.3 reshape.190
  94.6 55.5 %all-to-all-done.1 = bf16[16,54,2560]{2,1,0:T(8,128)(2,1)} async-done(((bf16[16,54,2560]{2,1,0:T(8,128)(2,1)}), bf16[16,54,2560]{2,1,0:T(8,128)(2,1)}, u32[]{:S(2)}, u32[]{:S(2)}) %all-to-all-start.1) | async-done | bytes 4423712 | tf_op jit(solution)/shard_map/all_to_all | solution.py:91
  150.1 4.5 all-to-all-start.2
  154.6 0.0 reduce-scatter.5.cloned.1.call-start
  154.7 0.1 reshape.172
  154.8 5.3 reshape.165
  160.1 60.6 %all-to-all-done.2 = bf16[16,54,2560]{2,1,0:T(8,128)(2,1)} async-done(((bf16[16,54,2560]{2,1,0:T(8,128)(2,1)}), bf16[16,54,2560]{2,1,0:T(8,128)(2,1)}, u32[]{:S(2)}, u32[]{:S(2)}) %all-to-all-start.2) | async-done | bytes 4423712 | tf_op jit(solution)/shard_map/all_to_all | solution.py:90
  220.7 5.3 reshape.166
  226.0 44.4 %all-gather.5.cloned.1.call-done = bf16[1,2560,1536]{2,1,0:T(8,128)(2,1)} async-done(((bf16[1,320,1536]{2,1,0:T(8,128)(2,1)}), bf16[1,2560,1536]{2,1,0:T(8,128)(2,1)}) %all-gather.5.cloned.1.call-update) | async-done | bytes 7864336 | tf_op jit(solution)/shard_map/all_gather | solution.py:84
  270.4 10.8 %fusion.2 = f32[864,1536]{1,0:T(8,128)S(1)} fusion(bf16[864,2560]{1,0:T(8,128)(2,1)} %reshape.166, bf16[1,2560,1536]{2,1,0:T(8,128)(2,1)} %all-gather.5.cloned.1.call-done), kind=kOutput, calls=%fused_computation.9 | convolution fusion | flops 6794772480 | bytes 17596416 | tf_op jit(solution)/shard_map/dot_general | solution.py:21
  281.2 2.3 copy-done.9
  283.5 6.2 convolution_convert_fusion.1
  289.7 0.0 reduce-scatter.5.cloned.1.call-update
  289.7 0.2 all-gather.3.cloned.1.call-start
  290.0 87.4 %reduce-scatter.5.cloned.1.call-done = bf16[96,2560]{1,0:T(8,128)(2,1)} async-done(((bf16[768,2560]{1,0:T(8,128)(2,1)}), bf16[96,2560]{1,0:T(8,128)(2,1)}) %reduce-scatter.5.cloned.1.call-update) | async-done | bytes 491536 | tf_op jit(solution)/shard_map/reduce_scatter | solution.py:127
  377.4 3.3 multiply_subtract_fusion.1
  380.7 0.0 all-gather.3.cloned.1.call-update
  380.7 0.0 reduce-scatter.3.cloned.1.call-start
  380.8 85.9 %all-gather.3.cloned.1.call-done = bf16[1,768,2560]{2,1,0:T(8,128)(2,1)} async-done(((bf16[1,96,2560]{2,1,0:T(8,128)(2,1)}), bf16[1,768,2560]{2,1,0:T(8,128)(2,1)}) %all-gather.3.cloned.1.call-update) | async-done | bytes 3932176 | tf_op jit(solution)/shard_map/all_gather | solution.py:85
  466.7 9.4 %multiply_convert_fusion.2 = (bf16[864,768]{1,0:T(8,128)(2,1)S(1)}, bf16[864,768]{1,0:T(8,128)(2,1)S(1)}, bf16[864]{0:T(1024)(128)(2,1)S(1)}) fusion(f32[864,1536]{1,0:T(8,128)} %copy-done.9, f32[864]{0:T(1024)S(1)} %reshape.172, bf16[864,2560]{1,0:T(8,128)(2,1)} %reshape.165, bf16[1,768,2560]{2,1,0:T(8,128)(2,1)} %all-gather.3.cloned.1.call-done), kind=kOutput, calls=%fused_computation.20 | convolution fusion | flops 3408665856 | bytes 16323648 | tf_op jit(solution)/shard_map/dot_general | solution.py:26
  476.1 12.8 %convolution_convert_fusion = bf16[2560,1536]{1,0:T(8,128)(2,1)} fusion(bf16[864,2560]{1,0:T(8,128)(2,1)} %reshape.166, bf16[864,768]{1,0:T(8,128)(2,1)S(1)} %get-tuple-element.33, bf16[864,768]{1,0:T(8,128)(2,1)S(1)} %get-tuple-element.32), kind=kOutput, calls=%fused_computation.6 | convolution fusion | flops 6804013056 | bytes 14942208 | tf_op jit(solution)/shard_map/dot_general | solution.py:119
  489.0 0.0 reduce-scatter.3.cloned.1.call-update
  489.0 0.7 convert_element_type.73
  489.7 7.3 %all-to-all-start.4 = ((bf16[16,1,54]{2,1,0:T(2,128)(2,1)}), bf16[16,1,54]{2,1,0:T(2,128)(2,1)S(1)}, u32[]{:S(2)}, u32[]{:S(2)}) async-start(bf16[16,1,54]{2,1,0:T(2,128)(2,1)} %convert_element_type.73), calls=%async_computation.4 | async-start | bytes 16384 | tf_op jit(solution)/shard_map/all_to_all | solution.py:110
  497.0 12.6 %fusion.4 = bf16[864,2560]{1,0:T(8,128)(2,1)} fusion(bf16[1,2560,1536]{2,1,0:T(8,128)(2,1)} %all-gather.5.cloned.1.call-done, bf16[864,768]{1,0:T(8,128)(2,1)S(1)} %get-tuple-element.33, bf16[864,768]{1,0:T(8,128)(2,1)S(1)} %get-tuple-element.32), kind=kOutput, calls=%fused_computation.11 | convolution fusion | flops 6802292736 | bytes 14942208 | tf_op jit(solution)/shard_map/dot_general | solution.py:36
  509.6 5.3 reshape.167
  515.0 0.0 all-to-all-done.4
  515.0 7.3 %all-to-all-start.3 = ((bf16[16,54,2560]{2,1,0:T(8,128)(2,1)}), bf16[16,54,2560]{2,1,0:T(8,128)(2,1)}, u32[]{:S(2)}, u32[]{:S(2)}) async-start(bf16[16,54,2560]{2,1,0:T(8,128)(2,1)} %reshape.167), calls=%async_computation.3 | async-start | bytes 9175040 | tf_op jit(solution)/shard_map/all_to_all | solution.py:109
  522.3 0.1 reshape.170
  522.4 5.0 gather_fusion.4
  527.4 0.1 reshape.171
  527.5 0.7 copy.31
  528.2 60.0 %all-to-all-done.3 = bf16[16,54,2560]{2,1,0:T(8,128)(2,1)} async-done(((bf16[16,54,2560]{2,1,0:T(8,128)(2,1)}), bf16[16,54,2560]{2,1,0:T(8,128)(2,1)}, u32[]{:S(2)}, u32[]{:S(2)}) %all-to-all-start.3) | async-done | bytes 4423712 | tf_op jit(solution)/shard_map/all_to_all | solution.py:109
  588.2 5.3 reshape.168
  593.6 11.3 %gather_fusion.3 = bf16[768,2560]{1,0:T(8,128)(2,1)} fusion(bf16[864,2560]{1,0:T(8,128)(2,1)} %reshape.168, s32[1024]{0:T(1024)S(1)} %pad_clamp_fusion), kind=kCustom, calls=%fused_computation.3 | custom fusion | bytes 7867392 | tf_op jit(solution)/shard_map/gather | solution.py:142
  604.8 7.2 %reshape.169 = bf16[128,6,2560]{2,1,0:T(8,128)(2,1)} reshape(bf16[768,2560]{1,0:T(8,128)(2,1)} %gather_fusion.3) | data formatting | bytes 7864320 | tf_op jit(solution)/shard_map/reshape | solution.py:144
  612.0 6.6 reduce_sum.34
  618.6 79.0 %reduce-scatter.3.cloned.1.call-done = bf16[320,1536]{1,0:T(8,128)(2,1)} async-done(((bf16[2560,1536]{1,0:T(8,128)(2,1)}), bf16[320,1536]{1,0:T(8,128)(2,1)}) %reduce-scatter.3.cloned.1.call-update) | async-done | bytes 983056 | tf_op jit(solution)/shard_map/reduce_scatter | solution.py:118
  697.6 6.0 multiply_subtract_fusion
  (31 shorter events, 0.3 us)
Async XLA Ops:
  7.2 2.7 copy-start.7
  7.2 3.2 copy-start.8
  7.2 263.2 %all-gather.5.cloned.1.call-start = ((), (), s32[]{:S(2)}) async-start(), calls=%async_computation.8 | async-start | bytes 8847360 | tf_op jit(solution)/shard_map/all_gather | solution.py:84
  50.6 15.2 %copy-start.5 = (bf16[128,2560]{1,0:T(8,128)(2,1)S(1)}, bf16[128,2560]{1,0:T(8,128)(2,1)}, u32[]{:S(2)}) copy-start(bf16[128,2560]{1,0:T(8,128)(2,1)} %param.11) | copy-start | bytes 1966084
  57.2 19.3 %all-to-all-start = ((bf16[16,1,54]{2,1,0:T(2,128)(2,1)}), bf16[16,1,54]{2,1,0:T(2,128)(2,1)S(1)}, u32[]{:S(2)}, u32[]{:S(2)}) async-start(bf16[16,1,54]{2,1,0:T(2,128)(2,1)} %all_to_all.25), calls=%async_computation | async-start | bytes 16384 | tf_op jit(solution)/shard_map/all_to_all | solution.py:92
  76.5 7.4 %copy-start.6 = (bf16[128,2560]{1,0:T(8,128)(2,1)S(1)}, bf16[128,2560]{1,0:T(8,128)(2,1)}, u32[]{:S(2)}) copy-start(bf16[128,2560]{1,0:T(8,128)(2,1)} %param.10) | copy-start | bytes 1966084
  76.5 73.6 %all-to-all-start.1 = ((bf16[16,54,2560]{2,1,0:T(8,128)(2,1)}), bf16[16,54,2560]{2,1,0:T(8,128)(2,1)}, u32[]{:S(2)}, u32[]{:S(2)}) async-start(bf16[16,54,2560]{2,1,0:T(8,128)(2,1)} %reshape.182), calls=%async_computation.1 | async-start | bytes 9175040 | tf_op jit(solution)/shard_map/all_to_all | solution.py:91
  150.1 70.5 %all-to-all-start.2 = ((bf16[16,54,2560]{2,1,0:T(8,128)(2,1)}), bf16[16,54,2560]{2,1,0:T(8,128)(2,1)}, u32[]{:S(2)}, u32[]{:S(2)}) async-start(bf16[16,54,2560]{2,1,0:T(8,128)(2,1)} %reshape.190), calls=%async_computation.2 | async-start | bytes 9175040 | tf_op jit(solution)/shard_map/all_to_all | solution.py:90
  154.6 222.8 %reduce-scatter.5.cloned.1.call-start = ((), (), s32[]{:S(2)}) async-start(), calls=%async_computation.10 | async-start | bytes 4423680 | tf_op jit(solution)/shard_map/reduce_scatter | solution.py:127
  270.4 13.1 %copy-start.1 = (bf16[864,2560]{1,0:T(8,128)(2,1)S(1)}, bf16[864,2560]{1,0:T(8,128)(2,1)}, u32[]{:S(2)}) copy-start(bf16[864,2560]{1,0:T(8,128)(2,1)} %reshape.165) | copy-start | bytes 13271044
  281.2 2.3 copy-start.9
  289.7 87.7 %copy-start.2 = (f32[1,96,2560]{2,1,0:T(8,128)S(1)}, f32[1,96,2560]{2,1,0:T(8,128)}, u32[]{:S(2)}) copy-start(f32[1,96,2560]{2,1,0:T(8,128)} %param.15) | copy-start | bytes 2949124
  289.7 87.7 %copy-start.3 = (f32[1,96,2560]{2,1,0:T(8,128)S(1)}, f32[1,96,2560]{2,1,0:T(8,128)}, u32[]{:S(2)}) copy-start(f32[1,96,2560]{2,1,0:T(8,128)} %param.17) | copy-start | bytes 2949124
  289.7 87.7 %copy-start.4 = (f32[1,96,2560]{2,1,0:T(8,128)S(1)}, f32[1,96,2560]{2,1,0:T(8,128)}, u32[]{:S(2)}) copy-start(f32[1,96,2560]{2,1,0:T(8,128)} %param.19) | copy-start | bytes 2949124
  289.7 176.9 %all-gather.3.cloned.1.call-start = ((), (), s32[]{:S(2)}) async-start(), calls=%async_computation.7 | async-start | bytes 4423680 | tf_op jit(solution)/shard_map/all_gather | solution.py:85
  380.7 316.9 %reduce-scatter.3.cloned.1.call-start = ((), (), s32[]{:S(2)}) async-start(), calls=%async_computation.9 | async-start | bytes 8847360 | tf_op jit(solution)/shard_map/reduce_scatter | solution.py:118
  489.7 25.3 %all-to-all-start.4 = ((bf16[16,1,54]{2,1,0:T(2,128)(2,1)}), bf16[16,1,54]{2,1,0:T(2,128)(2,1)S(1)}, u32[]{:S(2)}, u32[]{:S(2)}) async-start(bf16[16,1,54]{2,1,0:T(2,128)(2,1)} %convert_element_type.73), calls=%async_computation.4 | async-start | bytes 16384 | tf_op jit(solution)/shard_map/all_to_all | solution.py:110
  515.0 73.3 %all-to-all-start.3 = ((bf16[16,54,2560]{2,1,0:T(8,128)(2,1)}), bf16[16,54,2560]{2,1,0:T(8,128)(2,1)}, u32[]{:S(2)}, u32[]{:S(2)}) async-start(bf16[16,54,2560]{2,1,0:T(8,128)(2,1)} %reshape.167), calls=%async_computation.3 | async-start | bytes 9175040 | tf_op jit(solution)/shard_map/all_to_all | solution.py:109
  612.0 85.6 %copy-start = (f32[1,320,1536]{2,1,0:T(8,128)S(1)}, f32[1,320,1536]{2,1,0:T(8,128)}, u32[]{:S(2)}) copy-start(f32[1,320,1536]{2,1,0:T(8,128)} %param.14) | copy-start | bytes 5898244
Sparse Core Ops, SparseCore 0:
  10.2 260.0 all-gather.4
  289.9 87.4 reduce-scatter.4
  380.8 85.7 all-gather.2
  489.1 208.4 reduce-scatter.2
where the time goes:
time: 712 us; the launch traced here: 710 us
  waiting for transfers between devices  473 us (66%)
  local copies, waits for them, and re-layouts  116 us (16%)
  matrix products  51.9 us (7%)
  starting transfers between devices  35.2 us (5%)
  other arithmetic  20.5 us (3%)
  between operations  14 us (2%)
    reduce_scatter x1, waiting for transfers between devices, on_device(): lax.psum_scatter(lax.dot_general(columns, flat_grads, (((0,), (0,)), ((),...  87.4 us
    all_gather x1, waiting for transfers between devices, on_device(): lax.all_gather(weights_out.astype(jnp.bfloat16), 'dp', axis=1, tiled=True)  85.9 us
    reduce_scatter x1, waiting for transfers between devices, on_device(): lax.psum_scatter(lax.dot_general(columns, flat_pre, (((0,), (0,)), ((), (...  79 us
    all_to_all x1, waiting for transfers between devices, on_device(): lax.all_to_all(sent_tokens, 'expert', split_axis=0, concat_axis=0, tiled=...  60.6 us
    all_to_all x1, waiting for transfers between devices, on_device(): lax.all_to_all(row_grad, 'expert', split_axis=0, concat_axis=0, tiled=True)  60 us
    all_to_all x1, waiting for transfers between devices, on_device(): lax.all_to_all(sent_grads, 'expert', split_axis=0, concat_axis=0, tiled=T...  55.5 us
    all_gather x1, waiting for transfers between devices, on_device(): lax.all_gather(weights_in.astype(jnp.bfloat16), 'dp', axis=1, tiled=True)  44.4 us
    scatter x1, local copies, waits for them, and re-layouts, on_device(): slot_pick = jnp.full((experts, capacity), pick_total, jnp.int32).at[flat_...  37.7 us
  transfers between devices with their start and end apart: 9, of which 7 were waited for; matrix products, arithmetic and copies ran while one was open for 19% of the time, Pallas kernels for 0%

commit v1 on v0

--- a/solution.py
+++ b/solution.py
@@ -82,7 +82,12 @@
     ]
     gathered_in, gathered_out = (
         lax.all_gather(weights_in.astype(jnp.bfloat16), "dp", axis=1, tiled=True),
-        lax.all_gather(weights_out.astype(jnp.bfloat16), "dp", axis=1, tiled=True),
+        jnp.concatenate(
+            lax.all_to_all(
+                jnp.stack([weights_out.astype(jnp.bfloat16)] * lax.axis_size("dp")), "dp", 0, 0
+            ),
+            axis=1,
+        ),
     )
     wide_in = gathered_in[0]
     wide_out = gathered_out[0]

time: 712 us -> 669 us (0.940)
  waiting for transfers between devices: 473 us -> 387 us
  blocking collectives: 0 us -> 50.2 us
  matrix products: 51.9 us -> 44.4 us
    all_gather x1 -> x0, waiting for transfers between devices: 85.9 us -> none  [on_device(): lax.all_gather(weights_out.astype(jnp.bfloat16), 'dp', axis=1, tiled=True)]
    all_to_all x0 -> x1, blocking collectives: none -> 50.2 us  [on_device(): lax.all_to_all(jnp.stack([weights_out.astype(jnp.bfloat16)] * lax.axis_si...]
  transfers between devices with their start and end apart: 9 -> 8, of which waited for: 7 -> 6; matrix products, arithmetic and copies ran while one was open for 19% -> 20% of each run, Pallas kernels for 0% -> 0%
where the time goes in v1:
time: 669 us; the launch traced here: 668 us
  waiting for transfers between devices  387 us (58%)
  local copies, waits for them, and re-layouts  116 us (17%)
  blocking collectives  50.2 us (8%)
  matrix products  44.4 us (7%)
  starting transfers between devices  36.3 us (5%)
  other arithmetic  20.5 us (3%)
  between operations  14.1 us (2%)
    reduce_scatter x1, waiting for transfers between devices, on_device(): lax.psum_scatter(lax.dot_general(columns, flat_grads, (((0,), (0,)), ((),...  87.4 us
    reduce_scatter x1, waiting for transfers between devices, on_device(): lax.psum_scatter(lax.dot_general(columns, flat_pre, (((0,), (0,)), ((), (...  78.3 us
    all_to_all x1, waiting for transfers between devices, on_device(): lax.all_to_all(sent_tokens, 'expert', split_axis=0, concat_axis=0, tiled=...  60.6 us
    all_to_all x1, waiting for transfers between devices, on_device(): lax.all_to_all(row_grad, 'expert', split_axis=0, concat_axis=0, tiled=True)  60.3 us
    all_to_all x1, waiting for transfers between devices, on_device(): lax.all_to_all(sent_grads, 'expert', split_axis=0, concat_axis=0, tiled=T...  55.6 us
    all_to_all x1, blocking collectives, on_device(): lax.all_to_all(jnp.stack([weights_out.astype(jnp.bfloat16)] * lax.axis_si...  50.2 us
    all_gather x1, waiting for transfers between devices, on_device(): lax.all_gather(weights_in.astype(jnp.bfloat16), 'dp', axis=1, tiled=True)  44.4 us
    scatter x1, local copies, waits for them, and re-layouts, on_device(): slot_pick = jnp.full((experts, capacity), pick_total, jnp.int32).at[flat_...  37.7 us
  transfers between devices with their start and end apart: 8, of which 6 were waited for; matrix products, arithmetic and copies ran while one was open for 20% of the time, Pallas kernels for 0%

profile of v1, /device:TPU:1, one launch (start us, length us, event | category | flops | bytes accessed | tf_op | source)
XLA Modules:
  0.0 668.1 jit_solution(12283208647550889293)
XLA Ops:
  7.2 0.0 all-gather.2.cloned.1.call-start
  7.2 2.6 convert_element_type.66
  9.8 0.0 all-gather.2.cloned.1.call-update
  9.9 0.1 copy.25
  10.0 0.1 reshape.166
  10.1 0.1 eq.29
  10.3 0.1 eq.25
  10.4 0.1 copy.24
  10.5 0.2 reshape.165
  10.7 1.7 reduce-window.6
  12.4 0.3 slice_reduce_fusion
  12.7 0.1 fusion.19
  12.9 37.7 %scatter_fusion = s32[16,54]{1,0:T(8,128)S(1)} fusion(s32[16,54]{1,0:T(8,128)S(1)} %broadcast_in_dim.6, s32[768]{0:T(1024)S(1)} %get-tuple-element.25, s32[768]{0:T(1024)S(1)} %iota.11), kind=kCustom, calls=%fused_computation.5 | custom fusion | bytes 15360 | tf_op jit(solution)/shard_map/scatter | solution.py:74
  50.6 0.0 copy-start.5
  50.6 0.1 reshape.178
  50.7 5.8 gather_fusion
  56.5 0.7 all_to_all.29
  57.2 8.4 %all-to-all-start = ((bf16[16,1,54]{2,1,0:T(2,128)(2,1)}), bf16[16,1,54]{2,1,0:T(2,128)(2,1)S(1)}, u32[]{:S(2)}, u32[]{:S(2)}) async-start(bf16[16,1,54]{2,1,0:T(2,128)(2,1)} %all_to_all.29), calls=%async_computation | async-start | bytes 16384 | tf_op jit(solution)/shard_map/all_to_all | solution.py:97
  65.7 0.1 reshape.186
  65.8 5.3 gather_fusion.1
  71.1 5.4 reshape.185
  76.5 0.0 all-to-all-done
  76.5 7.4 %all-to-all-start.1 = ((bf16[16,54,2560]{2,1,0:T(8,128)(2,1)}), bf16[16,54,2560]{2,1,0:T(8,128)(2,1)}, u32[]{:S(2)}, u32[]{:S(2)}) async-start(bf16[16,54,2560]{2,1,0:T(8,128)(2,1)} %reshape.185), calls=%async_computation.1 | async-start | bytes 9175040 | tf_op jit(solution)/shard_map/all_to_all | solution.py:96
  83.9 5.3 gather_fusion.2
  89.2 5.3 reshape.193
  94.5 55.6 %all-to-all-done.1 = bf16[16,54,2560]{2,1,0:T(8,128)(2,1)} async-done(((bf16[16,54,2560]{2,1,0:T(8,128)(2,1)}), bf16[16,54,2560]{2,1,0:T(8,128)(2,1)}, u32[]{:S(2)}, u32[]{:S(2)}) %all-to-all-start.1) | async-done | bytes 4423712 | tf_op jit(solution)/shard_map/all_to_all | solution.py:96
  150.1 4.4 all-to-all-start.3
  154.5 0.0 reduce-scatter.5.cloned.1.call-start
  154.6 0.1 reshape.175
  154.7 5.3 reshape.168
  160.0 60.6 %all-to-all-done.3 = bf16[16,54,2560]{2,1,0:T(8,128)(2,1)} async-done(((bf16[16,54,2560]{2,1,0:T(8,128)(2,1)}), bf16[16,54,2560]{2,1,0:T(8,128)(2,1)}, u32[]{:S(2)}, u32[]{:S(2)}) %all-to-all-start.3) | async-done | bytes 4423712 | tf_op jit(solution)/shard_map/all_to_all | solution.py:95
  220.6 5.3 reshape.169
  226.0 44.4 %all-gather.2.cloned.1.call-done = bf16[1,2560,1536]{2,1,0:T(8,128)(2,1)} async-done(((bf16[1,320,1536]{2,1,0:T(8,128)(2,1)}), bf16[1,2560,1536]{2,1,0:T(8,128)(2,1)}) %all-gather.2.cloned.1.call-update) | async-done | bytes 7864336 | tf_op jit(solution)/shard_map/all_gather | solution.py:84
  270.4 10.8 %fusion.2 = f32[864,1536]{1,0:T(8,128)S(1)} fusion(bf16[864,2560]{1,0:T(8,128)(2,1)} %reshape.169, bf16[1,2560,1536]{2,1,0:T(8,128)(2,1)} %all-gather.2.cloned.1.call-done), kind=kOutput, calls=%fused_computation.9 | convolution fusion | flops 6794772480 | bytes 17596416 | tf_op jit(solution)/shard_map/dot_general | solution.py:21
  281.2 2.3 copy-done.9
  283.5 6.3 convolution_convert_fusion.1
  289.8 0.0 reduce-scatter.5.cloned.1.call-update
  289.8 0.2 reduce-scatter.3.cloned.1.call-start
  290.0 87.4 %reduce-scatter.5.cloned.1.call-done = bf16[96,2560]{1,0:T(8,128)(2,1)} async-done(((bf16[768,2560]{1,0:T(8,128)(2,1)}), bf16[96,2560]{1,0:T(8,128)(2,1)}) %reduce-scatter.5.cloned.1.call-update) | async-done | bytes 491536 | tf_op jit(solution)/shard_map/reduce_scatter | solution.py:132
  377.5 3.3 multiply_subtract_fusion.1
  380.8 0.3 stack.2
  381.1 0.0 slice-start.1
  381.1 0.0 slice-start.2
  381.1 50.2 %all_to_all.36 = bf16[8,1,96,2560]{3,2,1,0:T(8,128)(2,1)S(1)} all-to-all(bf16[8,1,96,2560]{3,2,1,0:T(8,128)(2,1)S(1)} %stack.2), channel_id=1, replica_groups=mesh['dp'=8,'expert'=16] {'dp'}, dimensions={0} | all-to-all | bytes 7864320 | tf_op jit(solution)/shard_map/all_to_all | solution.py:86
  431.3 0.0 slice-start.3
  431.3 4.5 multiply_convert_fusion.2
  435.8 10.6 %convolution_convert_fusion = bf16[2560,1536]{1,0:T(8,128)(2,1)} fusion(bf16[864,2560]{1,0:T(8,128)(2,1)S(1)} %bitcast.59, bf16[864,768]{1,0:T(8,128)(2,1)S(1)} %get-tuple-element.33, bf16[864,768]{1,0:T(8,128)(2,1)S(1)} %get-tuple-element.32), kind=kOutput, calls=%fused_computation.6 | convolution fusion | flops 6804013056 | bytes 14942208 | tf_op jit(solution)/shard_map/dot_general | solution.py:124
  446.4 0.0 reduce-scatter.3.cloned.1.call-update
  446.4 0.7 convert_element_type.76
  447.1 8.5 %all-to-all-start.5 = ((bf16[16,1,54]{2,1,0:T(2,128)(2,1)}), bf16[16,1,54]{2,1,0:T(2,128)(2,1)S(1)}, u32[]{:S(2)}, u32[]{:S(2)}) async-start(bf16[16,1,54]{2,1,0:T(2,128)(2,1)} %convert_element_type.76), calls=%async_computation.5 | async-start | bytes 16384 | tf_op jit(solution)/shard_map/all_to_all | solution.py:115
  455.6 12.3 %fusion.4 = bf16[864,2560]{1,0:T(8,128)(2,1)} fusion(bf16[1,2560,1536]{2,1,0:T(8,128)(2,1)} %all-gather.2.cloned.1.call-done, bf16[864,768]{1,0:T(8,128)(2,1)S(1)} %get-tuple-element.33, bf16[864,768]{1,0:T(8,128)(2,1)S(1)} %get-tuple-element.32), kind=kOutput, calls=%fused_computation.11 | convolution fusion | flops 6802292736 | bytes 14942208 | tf_op jit(solution)/shard_map/dot_general | solution.py:36
  467.9 5.3 reshape.170
  473.3 7.3 %all-to-all-start.4 = ((bf16[16,54,2560]{2,1,0:T(8,128)(2,1)}), bf16[16,54,2560]{2,1,0:T(8,128)(2,1)}, u32[]{:S(2)}, u32[]{:S(2)}) async-start(bf16[16,54,2560]{2,1,0:T(8,128)(2,1)} %reshape.170), calls=%async_computation.4 | async-start | bytes 9175040 | tf_op jit(solution)/shard_map/all_to_all | solution.py:114
  480.6 0.1 reshape.173
  480.7 5.0 gather_fusion.4
  485.7 0.1 reshape.174
  485.8 0.7 copy.31
  486.5 60.3 %all-to-all-done.4 = bf16[16,54,2560]{2,1,0:T(8,128)(2,1)} async-done(((bf16[16,54,2560]{2,1,0:T(8,128)(2,1)}), bf16[16,54,2560]{2,1,0:T(8,128)(2,1)}, u32[]{:S(2)}, u32[]{:S(2)}) %all-to-all-start.4) | async-done | bytes 4423712 | tf_op jit(solution)/shard_map/all_to_all | solution.py:114
  546.8 5.4 reshape.171
  552.2 11.2 %gather_fusion.3 = bf16[768,2560]{1,0:T(8,128)(2,1)} fusion(bf16[864,2560]{1,0:T(8,128)(2,1)} %reshape.171, s32[1024]{0:T(1024)S(1)} %pad_clamp_fusion), kind=kCustom, calls=%fused_computation.3 | custom fusion | bytes 7867392 | tf_op jit(solution)/shard_map/gather | solution.py:147
  563.4 7.2 %reshape.172 = bf16[128,6,2560]{2,1,0:T(8,128)(2,1)} reshape(bf16[768,2560]{1,0:T(8,128)(2,1)} %gather_fusion.3) | data formatting | bytes 7864320 | tf_op jit(solution)/shard_map/reshape | solution.py:149
  570.6 6.6 reduce_sum.34
  577.2 78.3 %reduce-scatter.3.cloned.1.call-done = bf16[320,1536]{1,0:T(8,128)(2,1)} async-done(((bf16[2560,1536]{1,0:T(8,128)(2,1)}), bf16[320,1536]{1,0:T(8,128)(2,1)}) %reduce-scatter.3.cloned.1.call-update) | async-done | bytes 983056 | tf_op jit(solution)/shard_map/reduce_scatter | solution.py:123
  655.5 6.0 multiply_subtract_fusion
  (45 shorter events, 0.3 us)
Async XLA Ops:
  7.2 2.7 copy-start.7
  7.2 3.2 copy-start.8
  7.2 263.2 %all-gather.2.cloned.1.call-start = ((), (), s32[]{:S(2)}) async-start(), calls=%async_computation.8 | async-start | bytes 8847360 | tf_op jit(solution)/shard_map/all_gather | solution.py:84
  50.6 15.2 %copy-start.5 = (bf16[128,2560]{1,0:T(8,128)(2,1)S(1)}, bf16[128,2560]{1,0:T(8,128)(2,1)}, u32[]{:S(2)}) copy-start(bf16[128,2560]{1,0:T(8,128)(2,1)} %param.11) | copy-start | bytes 1966084
  57.2 19.3 %all-to-all-start = ((bf16[16,1,54]{2,1,0:T(2,128)(2,1)}), bf16[16,1,54]{2,1,0:T(2,128)(2,1)S(1)}, u32[]{:S(2)}, u32[]{:S(2)}) async-start(bf16[16,1,54]{2,1,0:T(2,128)(2,1)} %all_to_all.29), calls=%async_computation | async-start | bytes 16384 | tf_op jit(solution)/shard_map/all_to_all | solution.py:97
  76.5 7.4 %copy-start.6 = (bf16[128,2560]{1,0:T(8,128)(2,1)S(1)}, bf16[128,2560]{1,0:T(8,128)(2,1)}, u32[]{:S(2)}) copy-start(bf16[128,2560]{1,0:T(8,128)(2,1)} %param.10) | copy-start | bytes 1966084
  76.5 73.6 %all-to-all-start.1 = ((bf16[16,54,2560]{2,1,0:T(8,128)(2,1)}), bf16[16,54,2560]{2,1,0:T(8,128)(2,1)}, u32[]{:S(2)}, u32[]{:S(2)}) async-start(bf16[16,54,2560]{2,1,0:T(8,128)(2,1)} %reshape.185), calls=%async_computation.1 | async-start | bytes 9175040 | tf_op jit(solution)/shard_map/all_to_all | solution.py:96
  150.1 70.5 %all-to-all-start.3 = ((bf16[16,54,2560]{2,1,0:T(8,128)(2,1)}), bf16[16,54,2560]{2,1,0:T(8,128)(2,1)}, u32[]{:S(2)}, u32[]{:S(2)}) async-start(bf16[16,54,2560]{2,1,0:T(8,128)(2,1)} %reshape.193), calls=%async_computation.3 | async-start | bytes 9175040 | tf_op jit(solution)/shard_map/all_to_all | solution.py:95
  154.5 222.9 %reduce-scatter.5.cloned.1.call-start = ((), (), s32[]{:S(2)}) async-start(), calls=%async_computation.10 | async-start | bytes 4423680 | tf_op jit(solution)/shard_map/reduce_scatter | solution.py:132
  270.4 13.1 %copy-start.1 = (bf16[864,2560]{1,0:T(8,128)(2,1)S(1)}, bf16[864,2560]{1,0:T(8,128)(2,1)}, u32[]{:S(2)}) copy-start(bf16[864,2560]{1,0:T(8,128)(2,1)} %reshape.168) | copy-start | bytes 13271044
  281.2 2.3 copy-start.9
  289.8 87.7 %copy-start.2 = (f32[1,96,2560]{2,1,0:T(8,128)S(1)}, f32[1,96,2560]{2,1,0:T(8,128)}, u32[]{:S(2)}) copy-start(f32[1,96,2560]{2,1,0:T(8,128)} %param.15) | copy-start | bytes 2949124
  289.8 87.7 %copy-start.3 = (f32[1,96,2560]{2,1,0:T(8,128)S(1)}, f32[1,96,2560]{2,1,0:T(8,128)}, u32[]{:S(2)}) copy-start(f32[1,96,2560]{2,1,0:T(8,128)} %param.17) | copy-start | bytes 2949124
  289.8 87.7 %copy-start.4 = (f32[1,96,2560]{2,1,0:T(8,128)S(1)}, f32[1,96,2560]{2,1,0:T(8,128)}, u32[]{:S(2)}) copy-start(f32[1,96,2560]{2,1,0:T(8,128)} %param.19) | copy-start | bytes 2949124
  289.8 365.7 %reduce-scatter.3.cloned.1.call-start = ((), (), s32[]{:S(2)}) async-start(), calls=%async_computation.9 | async-start | bytes 8847360 | tf_op jit(solution)/shard_map/reduce_scatter | solution.py:123
  377.5 53.8 %slice-start.4 = ((s8[5308416]{0:T(1024)(128)(4,1)}), s8[4194304]{0:T(1024)(128)(4,1)S(1)}, s32[]{:S(2)}) async-start(s8[5308416]{0:T(1024)(128)(4,1)} %bitcast.62), calls=%async_computation.15 | async-start | bytes 8388608
  380.8 50.5 %slice-start = ((s8[4423680]{0:T(1024)(128)(4,1)}), s8[4194304]{0:T(1024)(128)(4,1)S(1)}, s32[]{:S(2)}) async-start(s8[4423680]{0:T(1024)(128)(4,1)} %bitcast.56), calls=%async_computation.11 | async-start | bytes 8388608
  380.8 50.5 %slice-start.5 = ((s8[5308416]{0:T(1024)(128)(4,1)}), s8[1114112]{0:T(1024)(128)(4,1)S(1)}, s32[]{:S(2)}) async-start(s8[5308416]{0:T(1024)(128)(4,1)} %bitcast.62), calls=%async_computation.16 | async-start | bytes 2228224
  381.1 50.2 %slice-start.1 = ((s8[4423680]{0:T(1024)(128)(4,1)}), s8[229376]{0:T(1024)(128)(4,1)S(1)}, s32[]{:S(2)}) async-start(s8[4423680]{0:T(1024)(128)(4,1)} %bitcast.56), calls=%async_computation.12 | async-start | bytes 458752
  381.1 54.7 %slice-start.2 = ((s8[4423680]{0:T(1024)(128)(4,1)}), s8[4194304]{0:T(1024)(128)(4,1)S(1)}, s32[]{:S(2)}) async-start(s8[4423680]{0:T(1024)(128)(4,1)} %bitcast.58), calls=%async_computation.13 | async-start | bytes 8388608
  431.3 4.5 slice-start.3
  447.1 26.2 %all-to-all-start.5 = ((bf16[16,1,54]{2,1,0:T(2,128)(2,1)}), bf16[16,1,54]{2,1,0:T(2,128)(2,1)S(1)}, u32[]{:S(2)}, u32[]{:S(2)}) async-start(bf16[16,1,54]{2,1,0:T(2,128)(2,1)} %convert_element_type.76), calls=%async_computation.5 | async-start | bytes 16384 | tf_op jit(solution)/shard_map/all_to_all | solution.py:115
  473.3 73.6 %all-to-all-start.4 = ((bf16[16,54,2560]{2,1,0:T(8,128)(2,1)}), bf16[16,54,2560]{2,1,0:T(8,128)(2,1)}, u32[]{:S(2)}, u32[]{:S(2)}) async-start(bf16[16,54,2560]{2,1,0:T(8,128)(2,1)} %reshape.170), calls=%async_computation.4 | async-start | bytes 9175040 | tf_op jit(solution)/shard_map/all_to_all | solution.py:114
  570.6 84.9 %copy-start = (f32[1,320,1536]{2,1,0:T(8,128)S(1)}, f32[1,320,1536]{2,1,0:T(8,128)}, u32[]{:S(2)}) copy-start(f32[1,320,1536]{2,1,0:T(8,128)} %param.14) | copy-start | bytes 5898244
Sparse Core Ops, SparseCore 0:
  10.2 260.0 all-gather.1
  289.9 87.4 reduce-scatter.4
  446.5 208.9 reduce-scatter.2
